TPU v7x, 256 devices: a whole 4x4x8 slice. The times are simulated.
256 devices in a mesh: dp: 16 (over z, x_hi), ctx: 16 (over y, x_lo, core).
Axes of the slice: x: 4 (x_hi: 2, x_lo: 2; x = x_hi * 2 + x_lo), y: 4, z: 8, core: 2. Of those that a mesh axis runs over, the one named last changes fastest.
Arguments:
- query_rows: bfloat16 [16, 3584, 1024], P('dp', 'ctx'), may hold values from -48 to 48
- key_rows: bfloat16 [16, 3584, 128], P('dp', 'ctx'), may hold values from -4 to 4
- value_rows: bfloat16 [16, 3584, 128], P('dp', 'ctx'), may hold values from -5 to 5
- out_grad: bfloat16 [16, 3584, 1024], P('dp', 'ctx'), may hold values from -5 to 5
- doc_ids: int32 [16, 3584], P('dp'), may hold values from 0 to 7, never falling along the last dimension, each value on 1 to 2688 neighbouring positions
- matching: int32 [16], replicated, may hold values from 0 to 15, as said below
Outputs:
- attended: bfloat16 [16, 3584, 1024], P('dp', 'ctx')
- query_grad: bfloat16 [16, 3584, 1024], P('dp', 'ctx')
- key_grad: bfloat16 [16, 3584, 128], P('dp', 'ctx')
- value_grad: bfloat16 [16, 3584, 128], P('dp', 'ctx')
Inputs may be any that keep to these rules, and one draw needn't show every extreme that they name: matching[b] is b XOR m for one m of 1 to 15 shared by all b, so micro-batches come in pairs.
All inputs are finite; a program needn't handle non-finite values.
Results may differ from a plain program's by a relative error of at most 0.035.
Values may be sent and summed in bfloat16 or wider, within the bound.
No kernel may reach another device: no remote copies, remote signals or barrier semaphores. Data moves between devices by JAX's collectives and lax.ppermute only.
A program may use at most 64 MiB of HBM per device.

v0:
```python
import math

import jax
import jax.numpy as jnp
from jax import lax
from jax.sharding import PartitionSpec as P


def from_partner(shard, axis, apart):
    return lax.ppermute(shard, axis, [(i, i ^ 1 << apart) for i in range(lax.axis_size(axis))])


def swap_partner(block, matching, dp_size):
    flip_mask = jnp.bitwise_xor(matching[0], 0)
    for bit_index in range(dp_size.bit_length() - 1):
        other = from_partner(block, "dp", bit_index)
        taken = jnp.bitwise_and(jnp.right_shift(flip_mask, bit_index), 1) == 1
        block = jnp.where(taken, other, block)
    return block


def on_device(query_rows, key_rows, value_rows, out_grad, doc_ids, matching):
    ctx_size = lax.axis_size("ctx")
    dp_size = lax.axis_size("dp")
    span_index = lax.axis_index("ctx")
    row_count = query_rows.shape[1]
    head_width = key_rows.shape[2]
    head_count = query_rows.shape[2] // head_width
    feature_count = head_count * head_width
    score_scale = 1.0 / math.sqrt(head_width)
    is_last = span_index == ctx_size - 1
    stored = jnp.concatenate([query_rows[0], out_grad[0], key_rows[0], value_rows[0]], axis=1)
    arrived = swap_partner(stored, matching, dp_size)
    local_rows = jnp.where(is_last, arrived, stored)
    query_local = local_rows[:, :feature_count]
    grad_local = local_rows[:, feature_count : 2 * feature_count]
    pair_local = local_rows[:, 2 * feature_count :]
    every_pair = lax.all_gather(pair_local, "ctx", axis=0, tiled=True)
    query_heads = query_local.reshape(row_count, head_count, head_width).transpose(1, 0, 2)
    grad_heads = grad_local.reshape(row_count, head_count, head_width).transpose(1, 0, 2)
    doc_all = doc_ids[0]
    row_offset = span_index * row_count
    doc_query = lax.dynamic_slice_in_dim(doc_all, row_offset, row_count)
    pos_query = row_offset + jnp.arange(row_count, dtype=jnp.int32)

    def block_scores(block_index):
        start_row = block_index * row_count
        pair_block = lax.dynamic_slice_in_dim(every_pair, start_row, row_count, 0)
        key_block = pair_block[:, :head_width]
        value_block = pair_block[:, head_width:]
        doc_key = lax.dynamic_slice_in_dim(doc_all, start_row, row_count)
        pos_key = start_row + jnp.arange(row_count, dtype=jnp.int32)
        allowed = (pos_key[None, :] <= pos_query[:, None]) & (
            doc_key[None, :] == doc_query[:, None]
        )
        raw_scores = (
            jnp.einsum("hcd,kd->hck", query_heads, key_block, preferred_element_type=jnp.float32)
            * score_scale
        )
        masked = jnp.where(allowed[None], raw_scores, -jnp.inf)
        return (masked, key_block, value_block)

    def block_live(block_index):
        return block_index <= span_index

    def visit(step_fn, initial):

        def one_turn(turn, totals):
            block_index = span_index - turn
            wanted = block_live(block_index) & (block_index >= 0)
            return lax.cond(
                wanted,
                lambda inner: step_fn(jnp.maximum(block_index, 0), inner),
                lambda inner: inner,
                totals,
            )

        return lax.fori_loop(0, ctx_size, one_turn, initial)

    def stats_step(block_index, totals):
        row_top, row_sum = totals
        masked, _, _ = block_scores(block_index)
        new_top = jnp.maximum(row_top, jnp.max(masked, axis=-1))
        row_sum = row_sum * jnp.exp(row_top - new_top) + jnp.sum(
            jnp.exp(masked - new_top[..., None]), axis=-1
        )
        return (new_top, row_sum)

    start_top = jnp.full((head_count, row_count), -jnp.inf, jnp.float32)
    start_sum = jnp.zeros((head_count, row_count), jnp.float32)
    row_top, row_sum = visit(stats_step, (start_top, start_sum))
    log_total = row_top + jnp.log(row_sum)

    def output_step(block_index, totals):
        masked, _, value_block = block_scores(block_index)
        weights = jnp.exp(masked - log_total[..., None]).astype(jnp.bfloat16)
        return totals + jnp.einsum(
            "hck,kd->hcd", weights, value_block, preferred_element_type=jnp.float32
        )

    out_total = visit(output_step, jnp.zeros((head_count, row_count, head_width), jnp.float32))
    out_heads = out_total.astype(jnp.bfloat16)
    row_dot = jnp.sum(grad_heads.astype(jnp.float32) * out_heads.astype(jnp.float32), axis=-1)

    def grad_step(block_index, totals):
        query_total, pair_total = totals
        masked, key_block, value_block = block_scores(block_index)
        probs = jnp.exp(masked - log_total[..., None])
        weights = probs.astype(jnp.bfloat16)
        dprob = jnp.einsum(
            "hcd,kd->hck", grad_heads, value_block, preferred_element_type=jnp.float32
        )
        dscore = (probs * (dprob - row_dot[..., None])).astype(jnp.bfloat16)
        query_total = query_total + jnp.einsum(
            "hck,kd->hcd", dscore, key_block, preferred_element_type=jnp.float32
        )
        key_term = jnp.einsum(
            "hck,hcd->kd", dscore, query_heads, preferred_element_type=jnp.float32
        )
        value_term = jnp.einsum(
            "hck,hcd->kd", weights, grad_heads, preferred_element_type=jnp.float32
        )
        start_row = block_index * row_count
        earlier = lax.dynamic_slice_in_dim(pair_total, start_row, row_count, 0)
        updated = earlier + jnp.concatenate([key_term, value_term], axis=1)
        pair_total = lax.dynamic_update_slice_in_dim(pair_total, updated, start_row, 0)
        return (query_total, pair_total)

    start_query = jnp.zeros((head_count, row_count, head_width), jnp.float32)
    start_pairs = jnp.zeros((ctx_size * row_count, 2 * head_width), jnp.float32)
    query_total, pair_total = visit(grad_step, (start_query, start_pairs))
    pair_mine = lax.psum_scatter(pair_total, "ctx", scatter_dimension=0, tiled=True)
    key_grad = (score_scale * pair_mine[:, :head_width]).astype(jnp.bfloat16)
    value_grad = pair_mine[:, head_width:].astype(jnp.bfloat16)
    query_grad = (score_scale * query_total).astype(jnp.bfloat16)
    out_flat = out_heads.transpose(1, 0, 2).reshape(row_count, feature_count)
    query_flat = query_grad.transpose(1, 0, 2).reshape(row_count, feature_count)
    leaving = jnp.concatenate([out_flat, query_flat, key_grad, value_grad], axis=1)
    returned = swap_partner(leaving, matching, dp_size)
    final_rows = jnp.where(is_last, returned, leaving)
    return (
        final_rows[None, :, :feature_count],
        final_rows[None, :, feature_count : 2 * feature_count],
        final_rows[None, :, 2 * feature_count : 2 * feature_count + head_width],
        final_rows[None, :, 2 * feature_count + head_width :],
    )


def solution(mesh):
    return jax.shard_map(
        on_device,
        mesh=mesh,
        in_specs=(
            P("dp", "ctx", None),
            P("dp", "ctx", None),
            P("dp", "ctx", None),
            P("dp", "ctx", None),
            P("dp", None),
            P(),
        ),
        out_specs=(
            P("dp", "ctx", None),
            P("dp", "ctx", None),
            P("dp", "ctx", None),
            P("dp", "ctx", None),
        ),
        check_vma=False,
    )
```

profile of v0, /device:TPU:26, one launch (start us, length us, event | category | flops | bytes accessed | tf_op | source)
XLA Modules:
  0.0 598.8 jit_solution(2112949265670554676)
XLA Ops:
  8.6 2.2 collective-permute-start
  10.9 23.9 %collective-permute-done = bf16[224,2304]{1,0:T(8,128)(2,1)S(1)} collective-permute-done((bf16[224,2304]{1,0:T(8,128)(2,1)S(1)}, bf16[224,2304]{1,0:T(8,128)(2,1)S(1)}, u32[]{:S(2)}, u32[]{:S(2)}) %collective-permute-start) | collective-permute-done | bytes 1032224 | tf_op jit(solution)/shard_map/ppermute | solution.py:10
  37.1 21.9 %collective-permute-done.1 = bf16[224,2304]{1,0:T(8,128)(2,1)S(1)} collective-permute-done((bf16[224,2304]{1,0:T(8,128)(2,1)S(1)}, bf16[224,2304]{1,0:T(8,128)(2,1)S(1)}, u32[]{:S(2)}, u32[]{:S(2)}) %collective-permute-start.1) | collective-permute-done | bytes 1032224 | tf_op jit(solution)/shard_map/ppermute | solution.py:10
  59.1 3.4 collective-permute-start.2
  62.5 43.3 %collective-permute-done.2 = bf16[224,2304]{1,0:T(8,128)(2,1)S(1)} collective-permute-done((bf16[224,2304]{1,0:T(8,128)(2,1)S(1)}, bf16[224,2304]{1,0:T(8,128)(2,1)S(1)}, u32[]{:S(2)}, u32[]{:S(2)}) %collective-permute-start.2) | collective-permute-done | bytes 1032224 | tf_op jit(solution)/shard_map/ppermute | solution.py:10
  105.9 6.3 %collective-permute-start.3 = (bf16[224,2304]{1,0:T(8,128)(2,1)S(1)}, bf16[224,2304]{1,0:T(8,128)(2,1)S(1)}, u32[]{:S(2)}, u32[]{:S(2)}) collective-permute-start(bf16[224,2304]{1,0:T(8,128)(2,1)S(1)} %broadcast_select_fusion.5), channel_id=1, source_target_pairs={{0,128},{16,144},{32,160},{48,176},{64,192},{80,208},{96,224},{112... | collective-permute-start | bytes 3096584 | tf_op jit(solution)/shard_map/ppermute | solution.py:10
  112.3 45.0 %collective-permute-done.3 = bf16[224,2304]{1,0:T(8,128)(2,1)S(1)} collective-permute-done((bf16[224,2304]{1,0:T(8,128)(2,1)S(1)}, bf16[224,2304]{1,0:T(8,128)(2,1)S(1)}, u32[]{:S(2)}, u32[]{:S(2)}) %collective-permute-start.3) | collective-permute-done | bytes 1032224 | tf_op jit(solution)/shard_map/ppermute | solution.py:10
  159.8 32.8 %all-gather.2.cloned.1.call-done = bf16[3584,256]{1,0:T(8,128)(2,1)} async-done(((bf16[224,256]{1,0:T(8,128)(2,1)}), bf16[3584,256]{1,0:T(8,128)(2,1)}) %all-gather.2.cloned.1.call-update) | async-done | bytes 1835024 | tf_op jit(solution)/shard_map/all_gather | solution.py:38
  192.6 31.2 %while.49 = (s32[]{:T(128)}, f32[8,224]{1,0:T(8,128)S(1)}, f32[8,224]{1,0:T(8,128)S(1)}, s32[]{:T(128)}, s32[3584]{0:T(1024)S(1)}, /*index=5*/s32[224]{0:T(256)S...) while((s32[]{:T(128)}, f32[8,224]{1,0:T(8,128)S(1)}, ...), condition=%wide.region_5.6_spmd.clone, body=%wide.region_0.5_spmd.clone.sunk | while | flops 105724880 | bytes 3980373 | solution.py:78
  223.9 30.4 %while.50 = (s32[]{:T(128)}, f32[8,224,128]{2,1,0:T(8,128)S(1)}, s32[]{:T(128)}, s32[3584]{0:T(1024)S(1)}, s32[224]{0:T(256)S(1)}, /*index=5*/bf16[3584,256]{1,0...) while((s32[]{:T(128)}, f32[8,224,128]{2,1,0:T(8,128)S(1)}, ...), condition=%wide.region_9.10_spmd.clone, body=%wide.region_6.9_spmd.clone.sunk | while | flops 207506880 | bytes 2526781 | solution.py:78
  256.8 102.1 %while.51 = (s32[]{:T(128)}, f32[8,224,128]{2,1,0:T(8,128)S(1)}, f32[3584,256]{1,0:T(8,128)}, s32[]{:T(128)}, s32[3584]{0:T(1024)S(1)}, /*index=5*/s32[224]{0:T(...) while((s32[]{:T(128)}, f32[8,224,128]{2,1,0:T(8,128)S(1)}, ...), condition=%wide.region_14.15_spmd.clone, body=%wide.region_11.14_spmd.clone.sunk | while | flops 517107136 | bytes 12108961 | solution.py:78
  256.8 6.8 %conditional.11 = ((f32[8,224,128]{2,1,0:T(8,128)S(1)}, f32[3584,256]{1,0:T(8,128)})) conditional(s32[]{:T(128)} %convert_element_type.76, (f32[8,224,128]{2,1,0:T(8,128)S(1)}, f32[3584,256]{1,0:T(8,128)}) %tuple.133, (s32[]{:T(128)}, s32[]{:T(128)}, s32[3584]{0:T(1024)S(1)}, s32[224]{0:T(256)S(1)}, bf16[3584,256]{1,0:T(8,128)(2,1)}, ...), branch_computations={%region_12.12_spmd, %region_13.13_spmd} | conditional | flops 517107136 | bytes 12107774 | solution.py:71
  263.6 6.8 %conditional.11 = ((f32[8,224,128]{2,1,0:T(8,128)S(1)}, f32[3584,256]{1,0:T(8,128)})) conditional(s32[]{:T(128)} %convert_element_type.76, (f32[8,224,128]{2,1,0:T(8,128)S(1)}, f32[3584,256]{1,0:T(8,128)}) %tuple.133, (s32[]{:T(128)}, s32[]{:T(128)}, s32[3584]{0:T(1024)S(1)}, s32[224]{0:T(256)S(1)}, bf16[3584,256]{1,0:T(8,128)(2,1)}, ...), branch_computations={%region_12.12_spmd, %region_13.13_spmd} | conditional | flops 517107136 | bytes 12107774 | solution.py:71
  270.4 6.8 %conditional.11 = ((f32[8,224,128]{2,1,0:T(8,128)S(1)}, f32[3584,256]{1,0:T(8,128)})) conditional(s32[]{:T(128)} %convert_element_type.76, (f32[8,224,128]{2,1,0:T(8,128)S(1)}, f32[3584,256]{1,0:T(8,128)}) %tuple.133, (s32[]{:T(128)}, s32[]{:T(128)}, s32[3584]{0:T(1024)S(1)}, s32[224]{0:T(256)S(1)}, bf16[3584,256]{1,0:T(8,128)(2,1)}, ...), branch_computations={%region_12.12_spmd, %region_13.13_spmd} | conditional | flops 517107136 | bytes 12107774 | solution.py:71
  277.2 6.8 %conditional.11 = ((f32[8,224,128]{2,1,0:T(8,128)S(1)}, f32[3584,256]{1,0:T(8,128)})) conditional(s32[]{:T(128)} %convert_element_type.76, (f32[8,224,128]{2,1,0:T(8,128)S(1)}, f32[3584,256]{1,0:T(8,128)}) %tuple.133, (s32[]{:T(128)}, s32[]{:T(128)}, s32[3584]{0:T(1024)S(1)}, s32[224]{0:T(256)S(1)}, bf16[3584,256]{1,0:T(8,128)(2,1)}, ...), branch_computations={%region_12.12_spmd, %region_13.13_spmd} | conditional | flops 517107136 | bytes 12107774 | solution.py:71
  284.1 6.8 %conditional.11 = ((f32[8,224,128]{2,1,0:T(8,128)S(1)}, f32[3584,256]{1,0:T(8,128)})) conditional(s32[]{:T(128)} %convert_element_type.76, (f32[8,224,128]{2,1,0:T(8,128)S(1)}, f32[3584,256]{1,0:T(8,128)}) %tuple.133, (s32[]{:T(128)}, s32[]{:T(128)}, s32[3584]{0:T(1024)S(1)}, s32[224]{0:T(256)S(1)}, bf16[3584,256]{1,0:T(8,128)(2,1)}, ...), branch_computations={%region_12.12_spmd, %region_13.13_spmd} | conditional | flops 517107136 | bytes 12107774 | solution.py:71
  290.8 6.8 %conditional.11 = ((f32[8,224,128]{2,1,0:T(8,128)S(1)}, f32[3584,256]{1,0:T(8,128)})) conditional(s32[]{:T(128)} %convert_element_type.76, (f32[8,224,128]{2,1,0:T(8,128)S(1)}, f32[3584,256]{1,0:T(8,128)}) %tuple.133, (s32[]{:T(128)}, s32[]{:T(128)}, s32[3584]{0:T(1024)S(1)}, s32[224]{0:T(256)S(1)}, bf16[3584,256]{1,0:T(8,128)(2,1)}, ...), branch_computations={%region_12.12_spmd, %region_13.13_spmd} | conditional | flops 517107136 | bytes 12107774 | solution.py:71
  297.6 6.8 %conditional.11 = ((f32[8,224,128]{2,1,0:T(8,128)S(1)}, f32[3584,256]{1,0:T(8,128)})) conditional(s32[]{:T(128)} %convert_element_type.76, (f32[8,224,128]{2,1,0:T(8,128)S(1)}, f32[3584,256]{1,0:T(8,128)}) %tuple.133, (s32[]{:T(128)}, s32[]{:T(128)}, s32[3584]{0:T(1024)S(1)}, s32[224]{0:T(256)S(1)}, bf16[3584,256]{1,0:T(8,128)(2,1)}, ...), branch_computations={%region_12.12_spmd, %region_13.13_spmd} | conditional | flops 517107136 | bytes 12107774 | solution.py:71
  304.4 6.8 %conditional.11 = ((f32[8,224,128]{2,1,0:T(8,128)S(1)}, f32[3584,256]{1,0:T(8,128)})) conditional(s32[]{:T(128)} %convert_element_type.76, (f32[8,224,128]{2,1,0:T(8,128)S(1)}, f32[3584,256]{1,0:T(8,128)}) %tuple.133, (s32[]{:T(128)}, s32[]{:T(128)}, s32[3584]{0:T(1024)S(1)}, s32[224]{0:T(256)S(1)}, bf16[3584,256]{1,0:T(8,128)(2,1)}, ...), branch_computations={%region_12.12_spmd, %region_13.13_spmd} | conditional | flops 517107136 | bytes 12107774 | solution.py:71
  311.3 6.8 %conditional.11 = ((f32[8,224,128]{2,1,0:T(8,128)S(1)}, f32[3584,256]{1,0:T(8,128)})) conditional(s32[]{:T(128)} %convert_element_type.76, (f32[8,224,128]{2,1,0:T(8,128)S(1)}, f32[3584,256]{1,0:T(8,128)}) %tuple.133, (s32[]{:T(128)}, s32[]{:T(128)}, s32[3584]{0:T(1024)S(1)}, s32[224]{0:T(256)S(1)}, bf16[3584,256]{1,0:T(8,128)(2,1)}, ...), branch_computations={%region_12.12_spmd, %region_13.13_spmd} | conditional | flops 517107136 | bytes 12107774 | solution.py:71
  318.1 6.8 %conditional.11 = ((f32[8,224,128]{2,1,0:T(8,128)S(1)}, f32[3584,256]{1,0:T(8,128)})) conditional(s32[]{:T(128)} %convert_element_type.76, (f32[8,224,128]{2,1,0:T(8,128)S(1)}, f32[3584,256]{1,0:T(8,128)}) %tuple.133, (s32[]{:T(128)}, s32[]{:T(128)}, s32[3584]{0:T(1024)S(1)}, s32[224]{0:T(256)S(1)}, bf16[3584,256]{1,0:T(8,128)(2,1)}, ...), branch_computations={%region_12.12_spmd, %region_13.13_spmd} | conditional | flops 517107136 | bytes 12107774 | solution.py:71
  324.9 6.8 %conditional.11 = ((f32[8,224,128]{2,1,0:T(8,128)S(1)}, f32[3584,256]{1,0:T(8,128)})) conditional(s32[]{:T(128)} %convert_element_type.76, (f32[8,224,128]{2,1,0:T(8,128)S(1)}, f32[3584,256]{1,0:T(8,128)}) %tuple.133, (s32[]{:T(128)}, s32[]{:T(128)}, s32[3584]{0:T(1024)S(1)}, s32[224]{0:T(256)S(1)}, bf16[3584,256]{1,0:T(8,128)(2,1)}, ...), branch_computations={%region_12.12_spmd, %region_13.13_spmd} | conditional | flops 517107136 | bytes 12107774 | solution.py:71
  331.7 6.8 %conditional.11 = ((f32[8,224,128]{2,1,0:T(8,128)S(1)}, f32[3584,256]{1,0:T(8,128)})) conditional(s32[]{:T(128)} %convert_element_type.76, (f32[8,224,128]{2,1,0:T(8,128)S(1)}, f32[3584,256]{1,0:T(8,128)}) %tuple.133, (s32[]{:T(128)}, s32[]{:T(128)}, s32[3584]{0:T(1024)S(1)}, s32[224]{0:T(256)S(1)}, bf16[3584,256]{1,0:T(8,128)(2,1)}, ...), branch_computations={%region_12.12_spmd, %region_13.13_spmd} | conditional | flops 517107136 | bytes 12107774 | solution.py:71
  338.5 6.8 %conditional.11 = ((f32[8,224,128]{2,1,0:T(8,128)S(1)}, f32[3584,256]{1,0:T(8,128)})) conditional(s32[]{:T(128)} %convert_element_type.76, (f32[8,224,128]{2,1,0:T(8,128)S(1)}, f32[3584,256]{1,0:T(8,128)}) %tuple.133, (s32[]{:T(128)}, s32[]{:T(128)}, s32[3584]{0:T(1024)S(1)}, s32[224]{0:T(256)S(1)}, bf16[3584,256]{1,0:T(8,128)(2,1)}, ...), branch_computations={%region_12.12_spmd, %region_13.13_spmd} | conditional | flops 517107136 | bytes 12107774 | solution.py:71
  345.3 6.8 %conditional.11 = ((f32[8,224,128]{2,1,0:T(8,128)S(1)}, f32[3584,256]{1,0:T(8,128)})) conditional(s32[]{:T(128)} %convert_element_type.76, (f32[8,224,128]{2,1,0:T(8,128)S(1)}, f32[3584,256]{1,0:T(8,128)}) %tuple.133, (s32[]{:T(128)}, s32[]{:T(128)}, s32[3584]{0:T(1024)S(1)}, s32[224]{0:T(256)S(1)}, bf16[3584,256]{1,0:T(8,128)(2,1)}, ...), branch_computations={%region_12.12_spmd, %region_13.13_spmd} | conditional | flops 517107136 | bytes 12107774 | solution.py:71
  352.1 6.8 %conditional.11 = ((f32[8,224,128]{2,1,0:T(8,128)S(1)}, f32[3584,256]{1,0:T(8,128)})) conditional(s32[]{:T(128)} %convert_element_type.76, (f32[8,224,128]{2,1,0:T(8,128)S(1)}, f32[3584,256]{1,0:T(8,128)}) %tuple.133, (s32[]{:T(128)}, s32[]{:T(128)}, s32[3584]{0:T(1024)S(1)}, s32[224]{0:T(256)S(1)}, bf16[3584,256]{1,0:T(8,128)(2,1)}, ...), branch_computations={%region_12.12_spmd, %region_13.13_spmd} | conditional | flops 517107136 | bytes 12107774 | solution.py:71
  359.2 78.1 %reduce-scatter.2.cloned.1.call-done = f32[224,256]{1,0:T(8,128)} async-done(((f32[3584,256]{1,0:T(8,128)}), f32[224,256]{1,0:T(8,128)}) %reduce-scatter.2.cloned.1.call-update) | async-done | bytes 229392 | tf_op jit(solution)/shard_map/reduce_scatter | solution.py:132
  441.1 24.0 %collective-permute-done.4 = bf16[224,2304]{1,0:T(8,128)(2,1)S(1)} collective-permute-done((bf16[224,2304]{1,0:T(8,128)(2,1)S(1)}, bf16[224,2304]{1,0:T(8,128)(2,1)S(1)}, u32[]{:S(2)}, u32[]{:S(2)}) %collective-permute-start.4) | collective-permute-done | bytes 1032224 | tf_op jit(solution)/shard_map/ppermute | solution.py:10
  466.3 24.5 %collective-permute-done.5 = bf16[224,2304]{1,0:T(8,128)(2,1)S(1)} collective-permute-done((bf16[224,2304]{1,0:T(8,128)(2,1)S(1)}, bf16[224,2304]{1,0:T(8,128)(2,1)S(1)}, u32[]{:S(2)}, u32[]{:S(2)}) %collective-permute-start.5) | collective-permute-done | bytes 1032224 | tf_op jit(solution)/shard_map/ppermute | solution.py:10
  492.8 46.1 %collective-permute-done.6 = bf16[224,2304]{1,0:T(8,128)(2,1)S(1)} collective-permute-done((bf16[224,2304]{1,0:T(8,128)(2,1)S(1)}, bf16[224,2304]{1,0:T(8,128)(2,1)S(1)}, u32[]{:S(2)}, u32[]{:S(2)}) %collective-permute-start.6) | collective-permute-done | bytes 1032224 | tf_op jit(solution)/shard_map/ppermute | solution.py:10
  539.0 5.1 collective-permute-start.7
  544.1 45.8 %collective-permute-done.7 = bf16[224,2304]{1,0:T(8,128)(2,1)S(1)} collective-permute-done((bf16[224,2304]{1,0:T(8,128)(2,1)S(1)}, bf16[224,2304]{1,0:T(8,128)(2,1)S(1)}, u32[]{:S(2)}, u32[]{:S(2)}) %collective-permute-start.7) | collective-permute-done | bytes 1032224 | tf_op jit(solution)/shard_map/ppermute | solution.py:10
  (446 shorter events, 238.5 us)
Async XLA Ops:
  7.2 27.6 %copy-start = (bf16[1,224,1024]{2,1,0:T(8,128)(2,1)S(1)}, bf16[1,224,1024]{2,1,0:T(8,128)(2,1)}, u32[]{:S(2)}) copy-start(bf16[1,224,1024]{2,1,0:T(8,128)(2,1)} %param.21) | copy-start | bytes 1376260
  7.2 27.6 %copy-start.3 = (bf16[1,224,128]{2,1,0:T(8,128)(2,1)S(1)}, bf16[1,224,128]{2,1,0:T(8,128)(2,1)}, u32[]{:S(2)}) copy-start(bf16[1,224,128]{2,1,0:T(8,128)(2,1)} %param.20) | copy-start | bytes 172036
  7.2 27.6 %copy-start.4 = (bf16[1,224,128]{2,1,0:T(8,128)(2,1)S(1)}, bf16[1,224,128]{2,1,0:T(8,128)(2,1)}, u32[]{:S(2)}) copy-start(bf16[1,224,128]{2,1,0:T(8,128)(2,1)} %param.19) | copy-start | bytes 172036
  7.2 27.6 %copy-start.1 = (bf16[1,224,1024]{2,1,0:T(8,128)(2,1)S(1)}, bf16[1,224,1024]{2,1,0:T(8,128)(2,1)}, u32[]{:S(2)}) copy-start(bf16[1,224,1024]{2,1,0:T(8,128)(2,1)} %param.18) | copy-start | bytes 1376260
  7.2 3.6 copy-start.6
  7.2 185.4 %all-gather.2.cloned.1.call-start = ((), (), s32[]{:S(2)}) async-start(), calls=%async_computation.1 | async-start | bytes 1949696 | tf_op jit(solution)/shard_map/all_gather | solution.py:38
  8.6 26.1 %collective-permute-start = (bf16[224,2304]{1,0:T(8,128)(2,1)S(1)}, bf16[224,2304]{1,0:T(8,128)(2,1)S(1)}, u32[]{:S(2)}, u32[]{:S(2)}) collective-permute-start(bf16[224,2304]{1,0:T(8,128)(2,1)S(1)} %pad_maximum_fusion), channel_id=1, source_target_pairs={{0,16},{16,0},{32,48},{48,32},{64,80},{80,64},{96,112},{112,96},{1... | collective-permute-start | bytes 3096584 | tf_op jit(solution)/shard_map/ppermute | solution.py:10
  35.1 23.9 %collective-permute-start.1 = (bf16[224,2304]{1,0:T(8,128)(2,1)S(1)}, bf16[224,2304]{1,0:T(8,128)(2,1)S(1)}, u32[]{:S(2)}, u32[]{:S(2)}) collective-permute-start(bf16[224,2304]{1,0:T(8,128)(2,1)S(1)} %broadcast_select_fusion.1), channel_id=1, source_target_pairs={{0,32},{16,48},{32,0},{48,16},{64,96},{80,112},{96,64},{112,80},{1... | collective-permute-start | bytes 3096584 | tf_op jit(solution)/shard_map/ppermute | solution.py:10
  59.1 46.7 %collective-permute-start.2 = (bf16[224,2304]{1,0:T(8,128)(2,1)S(1)}, bf16[224,2304]{1,0:T(8,128)(2,1)S(1)}, u32[]{:S(2)}, u32[]{:S(2)}) collective-permute-start(bf16[224,2304]{1,0:T(8,128)(2,1)S(1)} %broadcast_select_fusion.3), channel_id=1, source_target_pairs={{0,64},{16,80},{32,96},{48,112},{64,0},{80,16},{96,32},{112,48},{1... | collective-permute-start | bytes 3096584 | tf_op jit(solution)/shard_map/ppermute | solution.py:10
  105.9 51.4 %collective-permute-start.3 = (bf16[224,2304]{1,0:T(8,128)(2,1)S(1)}, bf16[224,2304]{1,0:T(8,128)(2,1)S(1)}, u32[]{:S(2)}, u32[]{:S(2)}) collective-permute-start(bf16[224,2304]{1,0:T(8,128)(2,1)S(1)} %broadcast_select_fusion.5), channel_id=1, source_target_pairs={{0,128},{16,144},{32,160},{48,176},{64,192},{80,208},{96,224},{112... | collective-permute-start | bytes 3096584 | tf_op jit(solution)/shard_map/ppermute | solution.py:10
  157.3 1.0 copy-start.2
  158.3 1.2 copy-start.5
  159.4 278.0 %reduce-scatter.2.cloned.1.call-start = ((), (), s32[]{:S(2)}) async-start(), calls=%async_computation.2 | async-start | bytes 3899392 | tf_op jit(solution)/shard_map/reduce_scatter | solution.py:132
  439.2 25.8 %collective-permute-start.4 = (bf16[224,2304]{1,0:T(8,128)(2,1)S(1)}, bf16[224,2304]{1,0:T(8,128)(2,1)S(1)}, u32[]{:S(2)}, u32[]{:S(2)}) collective-permute-start(bf16[224,2304]{1,0:T(8,128)(2,1)S(1)} %pad_maximum_fusion.1), channel_id=1, source_target_pairs={{0,16},{16,0},{32,48},{48,32},{64,80},{80,64},{96,112},{112,96},{1... | collective-permute-start | bytes 3096584 | tf_op jit(solution)/shard_map/ppermute | solution.py:10
  465.3 25.5 %collective-permute-start.5 = (bf16[224,2304]{1,0:T(8,128)(2,1)S(1)}, bf16[224,2304]{1,0:T(8,128)(2,1)S(1)}, u32[]{:S(2)}, u32[]{:S(2)}) collective-permute-start(bf16[224,2304]{1,0:T(8,128)(2,1)S(1)} %broadcast_select_fusion), channel_id=1, source_target_pairs={{0,32},{16,48},{32,0},{48,16},{64,96},{80,112},{96,64},{112,80},{1... | collective-permute-start | bytes 3096584 | tf_op jit(solution)/shard_map/ppermute | solution.py:10
  490.9 47.9 %collective-permute-start.6 = (bf16[224,2304]{1,0:T(8,128)(2,1)S(1)}, bf16[224,2304]{1,0:T(8,128)(2,1)S(1)}, u32[]{:S(2)}, u32[]{:S(2)}) collective-permute-start(bf16[224,2304]{1,0:T(8,128)(2,1)S(1)} %broadcast_select_fusion.2), channel_id=1, source_target_pairs={{0,64},{16,80},{32,96},{48,112},{64,0},{80,16},{96,32},{112,48},{1... | collective-permute-start | bytes 3096584 | tf_op jit(solution)/shard_map/ppermute | solution.py:10
  539.0 50.9 %collective-permute-start.7 = (bf16[224,2304]{1,0:T(8,128)(2,1)S(1)}, bf16[224,2304]{1,0:T(8,128)(2,1)S(1)}, u32[]{:S(2)}, u32[]{:S(2)}) collective-permute-start(bf16[224,2304]{1,0:T(8,128)(2,1)S(1)} %broadcast_select_fusion.4), channel_id=1, source_target_pairs={{0,128},{16,144},{32,160},{48,176},{64,192},{80,208},{96,224},{112... | collective-permute-start | bytes 3096584 | tf_op jit(solution)/shard_map/ppermute | solution.py:10
Sparse Core Ops, SparseCore 0:
  159.5 33.0 all-gather.1
  359.1 78.2 reduce-scatter.1
where the time goes:
time: 603 us; the launch traced here: 599 us
  waiting for transfers between devices  385 us (64%)
  matrix products  119 us (20%)
  other arithmetic  42.4 us (7%)
  starting transfers between devices  23.6 us (4%)
  between operations  14.4 us (2%)
  local copies, waits for them, and re-layouts  10.6 us (2%)
    ppermute x8, waiting for transfers between devices, from_partner(): lax.ppermute(shard, axis, [(i, i ^ 1 << apart) for i in range(lax.axis_si...  274 us
    reduce_scatter x1, waiting for transfers between devices, on_device(): lax.psum_scatter(pair_total, 'ctx', scatter_dimension=0, tiled=True)  78.1 us
    dot_general x30, matrix products, block_scores(): jnp.einsum('hcd,kd->hck', query_heads, key_block, preferred_element_type=...  40.4 us
    all_gather x1, waiting for transfers between devices, on_device(): every_pair = lax.all_gather(pair_local, 'ctx', axis=0, tiled=True)  32.8 us
    dot_general x15, matrix products, output_step(): jnp.einsum('hck,kd->hcd', weights, value_block, preferred_element_type=jn...  25.9 us
    dynamic_update_slice x15, other arithmetic, grad_step(): lax.dynamic_update_slice_in_dim(pair_total, updated, start_row, 0)  25.1 us
    ppermute x8, starting transfers between devices, from_partner(): lax.ppermute(shard, axis, [(i, i ^ 1 << apart) for i in range(lax.axis_si...  23.5 us
    dot_general x15, matrix products, grad_step(): jnp.einsum('hck,kd->hcd', dscore, key_block, preferred_element_type=jnp.f...  20.5 us
  transfers between devices with their start and end apart: 10, of which 10 were waited for; matrix products, arithmetic and copies ran while one was open for 0% of the time, Pallas kernels for 0%

commit v1 on v0

v1 whole, which is shorter than its diff:
```python
import functools
import math

import jax
import jax.numpy as jnp
from jax import lax
from jax.experimental import pallas as pl
from jax.experimental.pallas import tpu as pltpu
from jax.sharding import PartitionSpec as P

TILE = 256
LANES = 256


def dot(a, b, ca, cb):
    return lax.dot_general(a, b, (((ca,), (cb,)), ((), ())), preferred_element_type=jnp.float32)


def attention_kernel(
    heads, width, span, scale,
    bounds, low, query, grad, pairs,
    out, dquery, dpairs,
    q_rows, g_cols, scores, weights, dscores, out_t, dq_t, top, total,
):
    rows = heads * span
    tiles = pairs.shape[0] // TILE
    chunks = [slice(r, r + LANES) for r in range(0, rows, LANES)]
    first, clear, full, last, offset = (bounds[i] for i in range(5))
    factor = scale * math.log2(math.e)

    for h in range(heads):
        q_rows[h * span : (h + 1) * span, :] = query[:, h * width : (h + 1) * width]
        g_cols_rows = grad[:, h * width : (h + 1) * width]
        dscores[h * span : (h + 1) * span, 0:width] = g_cols_rows
    top[...] = jnp.full(top.shape, -jnp.inf, jnp.float32)
    total[...] = jnp.zeros(total.shape, jnp.float32)
    out_t[...] = jnp.zeros(out_t.shape, jnp.float32)
    dq_t[...] = jnp.zeros(dq_t.shape, jnp.float32)

    def keys_at(t):
        return pl.ds(pl.multiple_of(t * TILE, TILE), TILE)

    def score_tile(t, masked):
        at = keys_at(t)
        key = pairs[at, 0:width]
        for c in chunks:
            s = dot(key, q_rows[c, :], 1, 1)
            if masked:
                place = t * TILE + lax.broadcasted_iota(jnp.int32, (TILE, LANES), 0)
                ok = (place >= low[0:1, c]) & (place <= low[1:2, c])
                s = jnp.where(ok, s, -jnp.inf)
            scores[at, c] = s
            top[:, c] = jnp.maximum(top[:, c], jnp.max(s.reshape(TILE // 8, 8, LANES), axis=0))

    @pl.loop(first, clear)
    def _(t):
        score_tile(t, True)

    @pl.loop(clear, full)
    def _(t):
        score_tile(t, False)

    @pl.loop(full, last)
    def _(t):
        score_tile(t, True)

    peak = jnp.max(top[...], axis=0, keepdims=True) * factor
    top[...] = jnp.broadcast_to(peak, top.shape)

    @pl.loop(first, last)
    def _(t):
        at = keys_at(t)
        value_t = pairs[at, width : 2 * width].T
        for c in chunks:
            p = jnp.exp2(scores[at, c] * factor - top[0:1, c])
            total[:, c] += jnp.sum(p.reshape(TILE // 8, 8, LANES), axis=0)
            pb = p.astype(jnp.bfloat16)
            weights[at, c] = pb
            out_t[:, c] += dot(value_t, pb, 1, 0)

    inverse = 1.0 / jnp.sum(total[...], axis=0, keepdims=True)
    for r in range(0, rows, 128):
        c = slice(r, r + 128)
        o = out_t[:, c] * inverse[:, c]
        g = (dscores[c, 0:width].T.astype(jnp.float32) * inverse[:, c]).astype(jnp.bfloat16)
        g_cols[:, c] = g
        top[0:1, c] = jnp.sum(g.astype(jnp.float32) * o, axis=0, keepdims=True)
        q_at = o.T.astype(jnp.bfloat16)
        weights_out(out, q_at, r, span, width)

    for t in range(tiles):
        @pl.when((t < first) | (t >= last))
        def _():
            dpairs[t * TILE : (t + 1) * TILE, :] = jnp.zeros((TILE, 2 * width), jnp.bfloat16)

    @pl.loop(first, last)
    def _(t):
        at = keys_at(t)
        key = pairs[at, 0:width]
        key_t = key.T
        value = pairs[at, width : 2 * width]
        for c in chunks:
            dp = dot(value, g_cols[:, c], 1, 0)
            ds = weights[at, c] * (dp - top[0:1, c]).astype(jnp.bfloat16)
            dscores[0:TILE, c] = ds
            dq_t[:, c] += dot(key_t, ds, 1, 0)
        dk = dot(dscores[0:TILE, :], q_rows[...], 1, 0)
        dv = dot(weights[at, :], g_cols[...], 1, 1)
        dpairs[at, 0:width] = (dk * scale).astype(jnp.bfloat16)
        dpairs[at, width : 2 * width] = dv.astype(jnp.bfloat16)

    for r in range(0, rows, 128):
        d = (dq_t[:, r : r + 128].T * scale).astype(jnp.bfloat16)
        weights_out(dquery, d, r, span, width)


def weights_out(ref, block, start, span, width):
    done = 0
    while done < block.shape[0]:
        h, at = divmod(start + done, span)
        n = min(block.shape[0] - done, span - at)
        ref[at : at + n, h * width : (h + 1) * width] = block[done : done + n, :]
        done += n


def attention(bounds, low, query, grad, pairs, width):
    span, features = query.shape
    heads = features // width
    rows, keys = heads * span, pairs.shape[0]
    kernel = functools.partial(attention_kernel, heads, width, span, 1.0 / math.sqrt(width))
    vmem = pl.BlockSpec(memory_space=pltpu.VMEM)
    return pl.pallas_call(
        kernel,
        out_shape=(
            jax.ShapeDtypeStruct((span, features), jnp.bfloat16),
            jax.ShapeDtypeStruct((span, features), jnp.bfloat16),
            jax.ShapeDtypeStruct((keys, 2 * width), jnp.bfloat16),
        ),
        in_specs=[pl.BlockSpec(memory_space=pltpu.SMEM), vmem, vmem, vmem, vmem],
        out_specs=(vmem, vmem, vmem),
        scratch_shapes=[
            pltpu.VMEM((rows, width), jnp.bfloat16),
            pltpu.VMEM((width, rows), jnp.bfloat16),
            pltpu.VMEM((keys, rows), jnp.float32),
            pltpu.VMEM((keys, rows), jnp.bfloat16),
            pltpu.VMEM((rows, rows), jnp.bfloat16),
            pltpu.VMEM((width, rows), jnp.float32),
            pltpu.VMEM((width, rows), jnp.float32),
            pltpu.VMEM((8, rows), jnp.float32),
            pltpu.VMEM((8, rows), jnp.float32),
        ],
        compiler_params=pltpu.CompilerParams(vmem_limit_bytes=58 * 1024 * 1024),
        cost_estimate=pl.CostEstimate(
            flops=12 * rows * keys * width // 2, bytes_accessed=6 << 20, transcendentals=rows * keys // 2
        ),
        name="attention",
    )(bounds, low, query, grad, pairs)


def across(block, matching, dp_size):
    def turn(mask):
        return lambda v: lax.ppermute(v, "dp", [(i, i ^ mask) for i in range(dp_size)])

    return lax.switch(matching[0] - 1, [turn(mask) for mask in range(1, dp_size)], block)


def on_device(query_rows, key_rows, value_rows, out_grad, doc_ids, matching):
    ctx_size = lax.axis_size("ctx")
    dp_size = lax.axis_size("dp")
    me = lax.axis_index("ctx")
    span = query_rows.shape[1]
    width = key_rows.shape[2]
    heads = query_rows.shape[2] // width
    is_last = me == ctx_size - 1
    docs = doc_ids[0]
    offset = me * span

    docs_count = 8
    names = jnp.arange(docs_count, dtype=jnp.int32)[:, None]
    starts = jnp.sum((docs[None, :] < names).astype(jnp.int32), axis=1, keepdims=True)

    def low_of(part):
        return jnp.sum(jnp.where(part[None, :] == names, starts, 0), axis=0)

    low_mine = low_of(lax.dynamic_slice_in_dim(docs, offset, span))
    low_tail = low_of(docs[-span:])
    stored = jnp.concatenate([key_rows[0], value_rows[0]], axis=1)
    extra = jnp.stack([low_tail // 64, low_tail % 64]).astype(jnp.bfloat16)
    extra = jnp.pad(extra, ((0, 14), (0, 2 * width - span)))
    arrived = across(jnp.concatenate([stored, extra], axis=0), matching, dp_size)
    low_sent = arrived[span : span + 2, :span].astype(jnp.int32)
    low = jnp.where(is_last, low_sent[0] * 64 + low_sent[1], low_mine)
    to_last = jnp.where(is_last, stored, arrived[:span])
    sending = jnp.concatenate(
        [jnp.broadcast_to(stored[None], (ctx_size - 1,) + stored.shape), to_last[None]], axis=0
    )
    pairs = lax.all_to_all(sending, "ctx", 0, 0).reshape(ctx_size * span, 2 * width)

    end = offset + span
    first = low[0] // TILE
    last = (end + TILE - 1) // TILE
    clear = jnp.minimum((low[span - 1] + TILE - 1) // TILE, last)
    full = jnp.maximum((offset + 1) // TILE, clear)
    bounds = jnp.stack([first, clear, full, last, offset]).astype(jnp.int32)
    place = offset + jnp.arange(span, dtype=jnp.int32)
    limits = jnp.tile(jnp.stack([low, place]), (1, heads))

    out, dquery, dpairs = attention(bounds, limits, query_rows[0], out_grad[0], pairs, width)
    terms = lax.all_to_all(dpairs.reshape(ctx_size, span, 2 * width), "ctx", 0, 0)
    own = jnp.sum(terms[: ctx_size - 1].astype(jnp.float32), axis=0)
    tail = terms[ctx_size - 1]
    back = across(tail, matching, dp_size)
    final = jnp.where(
        is_last, tail.astype(jnp.float32), own + back.astype(jnp.float32)
    ).astype(jnp.bfloat16)
    return out[None], dquery[None], final[None, :, :width], final[None, :, width:]


def solution(mesh):
    rows = P("dp", "ctx", None)
    return jax.shard_map(
        on_device,
        mesh=mesh,
        in_specs=(rows, rows, rows, rows, P("dp", None), P()),
        out_specs=(rows, rows, rows, rows),
        check_vma=False,
    )
```

time: 603 us -> 130 us (0.22)
  the two profiles are of different devices: /device:TPU:26 before, /device:TPU:2 now
where the time goes in v1:
time: 130 us; the launch traced here: 128 us
  blocking collectives  52.2 us (40%)
  waiting for transfers between devices  26.7 us (21%)
  starting transfers between devices  23.3 us (18%)
  Pallas kernels  10.1 us (8%)
  other arithmetic  6.18 us (5%)
  local copies, waits for them, and re-layouts  4.75 us (4%)
  between operations  4.63 us (4%)
    all_to_all x1, blocking collectives, on_device(): lax.all_to_all(dpairs.reshape(ctx_size, span, 2 * width), 'ctx', 0, 0)  52.2 us
    all_to_all x1, waiting for transfers between devices, on_device(): lax.all_to_all(sending, 'ctx', 0, 0).reshape(ctx_size * span, 2 * width)  17.9 us
    ppermute x2, starting transfers between devices, turn(): lax.ppermute(v, 'dp', [(i, i ^ mask) for i in range(dp_size)])  17.3 us
    pallas_call x1, Pallas kernels, attention(): pl.pallas_call(kernel, out_shape=(jax.ShapeDtypeStruct((span, features),...  10.1 us
    ppermute x2, waiting for transfers between devices, turn(): lax.ppermute(v, 'dp', [(i, i ^ mask) for i in range(dp_size)])  8.75 us
    all_to_all x1, starting transfers between devices, on_device(): lax.all_to_all(sending, 'ctx', 0, 0).reshape(ctx_size * span, 2 * width)  5.94 us
  transfers between devices with their start and end apart: 3, of which 3 were waited for; matrix products, arithmetic and copies ran while one was open for 2% of the time, Pallas kernels for 0%

profile of v1, /device:TPU:2, one launch (start us, length us, event | category | flops | bytes accessed | tf_op | source)
XLA Modules:
  0.0 127.8 jit_solution(5930225960981316707)
XLA Ops:
  0.6 0.8 reduce
  1.4 0.8 fusion.9
  2.2 0.1 convert_reduce_fusion.1
  2.3 0.1 select_reduce_fusion
  3.1 0.9 pad_maximum_fusion.1
  4.0 11.6 %conditional.5 = (bf16[240,256]{1,0:T(8,128)(2,1)}) conditional(s32[]{:T(128)} %bitcast, bf16[240,256]{1,0:T(8,128)(2,1)S(1)} %pad_maximum_fusion.1, bf16[240,256]{1,0:T(8,128)(2,1)S(1)} %pad_maximum_fusion.1, bf16[240,256]{1,0:T(8,128)(2,1)S(1)} %pad_maximum_fusion.1, ...), branch_computations={%region_2.3_spmd, %region_3.4_spmd, %region_4.5_spmd, %region_5.6_... | conditional | bytes 491568 | solution.py:164
  4.0 6.4 %collective-permute-start.11 = (bf16[240,256]{1,0:T(8,128)(2,1)S(1)}, bf16[240,256]{1,0:T(8,128)(2,1)}, u32[]{:S(2)}, u32[]{:S(2)}) collective-permute-start(bf16[240,256]{1,0:T(8,128)(2,1)S(1)} %param.11), channel_id=1, source_target_pairs={{0,192},{16,208},{32,224},{48,240},{64,128},{80,144},{96,160},{112... | collective-permute-start | bytes 368648 | tf_op jit(solution)/shard_map/cond/branch_11_fun/ppermute | solution.py:162
  10.4 5.2 %collective-permute-done.11 = bf16[240,256]{1,0:T(8,128)(2,1)} collective-permute-done((bf16[240,256]{1,0:T(8,128)(2,1)S(1)}, bf16[240,256]{1,0:T(8,128)(2,1)}, u32[]{:S(2)}, u32[]{:S(2)}) %collective-permute-start.11) | collective-permute-done | bytes 122912 | tf_op jit(solution)/shard_map/cond/branch_11_fun/ppermute | solution.py:162
  15.6 1.0 pad_maximum_fusion.2
  16.6 0.2 broadcast_in_dim.43
  16.8 1.4 %pad_maximum_fusion = bf16[16,224,256]{2,1,0:T(8,128)(2,1)} fusion(bf16[1,224,256]{2,1,0:T(8,128)(2,1)S(1)} %get-tuple-element.87, bf16[15,224,256]{2,1,0:T(8,128)(2,1)S(1)} %broadcast_in_dim.43), kind=kLoop, calls=%fused_computation.1 | loop fusion | flops 917504 | bytes 3670016 | tf_op jit(solution)/shard_map/concatenate | solution.py:194
  18.2 5.9 %all-to-all-start = ((bf16[16,224,256]{2,1,0:T(8,128)(2,1)}), bf16[16,224,256]{2,1,0:T(8,128)(2,1)S(1)}, u32[]{:S(2)}, u32[]{:S(2)}) async-start(bf16[16,224,256]{2,1,0:T(8,128)(2,1)} %pad_maximum_fusion), calls=%async_computation | async-start | bytes 3670016 | tf_op jit(solution)/shard_map/all_to_all | solution.py:197
  24.1 0.7 slice_convert_fusion
  24.8 0.6 fusion.10
  28.7 0.7 tile.10.low
  29.4 0.6 stack.35.bounds
  30.0 17.9 %all-to-all-done = bf16[16,224,256]{2,1,0:T(8,128)(2,1)S(1)} async-done(((bf16[16,224,256]{2,1,0:T(8,128)(2,1)}), bf16[16,224,256]{2,1,0:T(8,128)(2,1)S(1)}, u32[]{:S(2)}, u32[]{:S(2)}) %all-to-all-start) | async-done | bytes 1835040 | tf_op jit(solution)/shard_map/all_to_all | solution.py:197
  48.0 0.0 copy-start
  48.0 1.3 copy-done
  49.2 10.1 %attention.1 = (bf16[224,1024]{1,0:T(8,128)(2,1)}, bf16[224,1024]{1,0:T(8,128)(2,1)}, bf16[3584,256]{1,0:T(8,128)(2,1)}) custom-call(s32[5]{0:T(128)} %stack.35.bounds, s32[2,1792]{1,0:T(2,128)} %tile.10.low, bf16[224,1024]{1,0:T(8,128)(2,1)} %bitcast.43, bf16[224,1024]{1,0:T(8,128)(2,1)} %bitcast.44, bf16[3584,256]{1,0:T(8,128)(2,1)} %bitcast.32), custom_call_target="tpu_custom_call" | custom-call | flops 4932501504 | bytes 6291456 | tf_op jit(solution)/shard_map/attention/pallas_call | solution.py:132
  59.4 52.2 %all_to_all.10 = bf16[16,224,256]{2,1,0:T(8,128)(2,1)S(1)} all-to-all(bf16[16,224,256]{2,1,0:T(8,128)(2,1)} %bitcast.33), channel_id=1, replica_groups=mesh['dp'=16,'ctx'=16] {'ctx'}, dimensions={0} | all-to-all | bytes 3670016 | tf_op jit(solution)/shard_map/all_to_all | solution.py:209
  111.5 14.5 %conditional.6 = (bf16[224,256]{1,0:T(8,128)(2,1)}) conditional(s32[]{:T(128)} %bitcast, bf16[224,256]{1,0:T(8,128)(2,1)S(1)} %slice_bitcast_fusion, bf16[224,256]{1,0:T(8,128)(2,1)S(1)} %slice_bitcast_fusion, bf16[224,256]{1,0:T(8,128)(2,1)S(1)} %slice_bitcast_fusion, ...), branch_computations={%region_19.20_spmd, %region_20.21_spmd, %region_21.22_spmd, %regio... | conditional | bytes 458800
  111.6 10.9 %collective-permute-start.26 = (bf16[224,256]{1,0:T(8,128)(2,1)S(1)}, bf16[224,256]{1,0:T(8,128)(2,1)}, u32[]{:S(2)}, u32[]{:S(2)}) collective-permute-start(bf16[224,256]{1,0:T(8,128)(2,1)S(1)} %param.26), channel_id=1, source_target_pairs={{0,192},{16,208},{32,224},{48,240},{64,128},{80,144},{96,160},{112... | collective-permute-start | bytes 344072 | tf_op jit(solution)/shard_map/cond/branch_11_fun/ppermute | solution.py:162
  122.5 3.5 %collective-permute-done.26 = bf16[224,256]{1,0:T(8,128)(2,1)} collective-permute-done((bf16[224,256]{1,0:T(8,128)(2,1)S(1)}, bf16[224,256]{1,0:T(8,128)(2,1)}, u32[]{:S(2)}, u32[]{:S(2)}) %collective-permute-start.26) | collective-permute-done | bytes 114720 | tf_op jit(solution)/shard_map/cond/branch_11_fun/ppermute | solution.py:162
  126.0 0.2 convert_reduce_fusion
  126.2 0.9 select_convert_fusion
  127.2 0.6 slice_bitcast_fusion.1
  (8 shorter events, 0.1 us)
Async XLA Ops:
  4.0 11.6 %collective-permute-start.11 = (bf16[240,256]{1,0:T(8,128)(2,1)S(1)}, bf16[240,256]{1,0:T(8,128)(2,1)}, u32[]{:S(2)}, u32[]{:S(2)}) collective-permute-start(bf16[240,256]{1,0:T(8,128)(2,1)S(1)} %param.11), channel_id=1, source_target_pairs={{0,192},{16,208},{32,224},{48,240},{64,128},{80,144},{96,160},{112... | collective-permute-start | bytes 368648 | tf_op jit(solution)/shard_map/cond/branch_11_fun/ppermute | solution.py:162
  18.2 29.8 %all-to-all-start = ((bf16[16,224,256]{2,1,0:T(8,128)(2,1)}), bf16[16,224,256]{2,1,0:T(8,128)(2,1)S(1)}, u32[]{:S(2)}, u32[]{:S(2)}) async-start(bf16[16,224,256]{2,1,0:T(8,128)(2,1)} %pad_maximum_fusion), calls=%async_computation | async-start | bytes 3670016 | tf_op jit(solution)/shard_map/all_to_all | solution.py:197
  48.0 1.3 copy-start
  111.6 14.5 %collective-permute-start.26 = (bf16[224,256]{1,0:T(8,128)(2,1)S(1)}, bf16[224,256]{1,0:T(8,128)(2,1)}, u32[]{:S(2)}, u32[]{:S(2)}) collective-permute-start(bf16[224,256]{1,0:T(8,128)(2,1)S(1)} %param.26), channel_id=1, source_target_pairs={{0,192},{16,208},{32,224},{48,240},{64,128},{80,144},{96,160},{112... | collective-permute-start | bytes 344072 | tf_op jit(solution)/shard_map/cond/branch_11_fun/ppermute | solution.py:162
